TPU v7x, 32 devices: a whole 2x2x4 slice. The times are simulated.
32 devices in a mesh: groups: 2 (over y), row: 4 (over x, core), col: 4 (over z).
Axes of the slice: x: 2, y: 2, z: 4, core: 2. Of those that a mesh axis runs over, the one named last changes fastest.
Arguments:
- tokens: float32 [512, 16384], P(('groups', 'col'), 'row'), parts along dimension 0, may hold values from -6 to 6
- weight: float32 [16384, 16384], P('row', 'col'), may hold values from -0.046875 to 0.046875
- token_amax: float32 [8, 4, 16], P('groups', 'row'), parts along dimension 0, may hold values from 0.25 to 3
- token_window: int32 [8, 4], P('groups', 'row'), parts along dimension 0, may hold values from 1 to 16
- weight_amax: float32 [4, 4, 16], P('row', 'col'), may hold values from 0.002 to 0.025
- weight_window: int32 [4, 4], P('row', 'col'), may hold values from 1 to 16
Outputs:
- projected: bfloat16 [512, 16384], P(('groups', 'row'), 'col'), parts along dimension 0
There are 2 independent parts, one for each index of `groups`. A program takes and returns all parts, laid end to end along the dimension named above; an argument that names none is the same for every part. Nothing has to cross between parts.
Inputs may be any that keep to these rules, and one draw needn't show every extreme that they name: `token_window`: the number of newest history entries that a block's scale uses. `weight_window`: the number of newest history entries that a tile's scale uses.
All inputs are finite; a program needn't handle non-finite values.
Results may differ from a plain program's by a relative error of at most 0.0056.
Values may be sent and summed in bfloat16 or wider, within the bound.
A program may use at most 192 MiB of HBM per device.

v0:
```python
import jax
import jax.numpy as jnp
from jax import lax
from jax.sharding import PartitionSpec as P

TOK_DEV = 64


QMAX = 448.0


def delayed_scale(history, window):
    hlen = history.shape[-1]
    position = jnp.arange(hlen, dtype=jnp.int32)
    keep = position >= (hlen - window)[..., None]
    amax = jnp.max(jnp.where(keep, history, jnp.float32(0.0)), axis=-1)
    return QMAX / amax


def quantize(values, scale):
    return jnp.clip(values * scale, -QMAX, QMAX).astype(jnp.bfloat16)


def row_descale(table, count):
    block_of = jnp.arange(count, dtype=jnp.int32) // TOK_DEV
    owners = jnp.arange(table.shape[0], dtype=jnp.int32)
    onehot = block_of[:, None] == owners[None, :]
    return jnp.sum(jnp.where(onehot, table[None, :], jnp.float32(0.0)), axis=1)


def shards(tokens, weight, token_amax, token_window, weight_amax, weight_window):
    token_scale = delayed_scale(token_amax[:, 0, :], token_window[:, 0])
    own_scale = lax.dynamic_index_in_dim(token_scale, lax.axis_index("col"), 0, keepdims=False)
    tile_scale = delayed_scale(weight_amax[0, 0, :], weight_window[0, 0])
    token_q = quantize(tokens, own_scale)
    weight_q = quantize(weight, tile_scale)
    table = 1.0 / (token_scale * tile_scale)
    piece = lax.all_gather(token_q, "col", axis=0, tiled=True)
    values = jnp.dot(piece, weight_q, preferred_element_type=jnp.float32)
    partial_sum = values * row_descale(table, piece.shape[0])[:, None]
    summed = lax.psum_scatter(partial_sum, "row", scatter_dimension=0, tiled=True)
    return summed.astype(jnp.bfloat16)


def solution(mesh):
    return jax.shard_map(
        shards,
        mesh=mesh,
        in_specs=(
            P(("groups", "col"), "row"),
            P("row", "col"),
            P("groups", "row", None),
            P("groups", "row"),
            P("row", "col", None),
            P("row", "col"),
        ),
        out_specs=P(("groups", "row"), "col"),
        check_vma=False,
    )
```

profile of v0, /device:TPU:16, one launch (start us, length us, event | category | flops | bytes accessed | tf_op | source)
XLA Modules:
  0.0 139.2 jit_solution(14560400240412649649)
XLA Ops:
  6.5 0.0 all-gather.2.cloned.1.call-start
  7.2 0.7 subtract_bitcast_fusion
  7.8 1.3 fusion.5
  9.9 0.9 select_reduce_fusion.1
  10.8 0.7 dynamic_slice.4
  11.5 2.8 %clamp_convert_fusion.4 = bf16[64,4096]{1,0:T(8,128)(2,1)} fusion(f32[64,4096]{1,0:T(8,128)} %param.6, f32[]{:T(128)} %bitcast.2), kind=kLoop, calls=%fused_computation.6 | loop fusion | flops 786432 | bytes 1572868 | tf_op jit(solution)/shard_map/convert_element_type | solution.py:21
  14.3 0.0 all-gather.2.cloned.1.call-update
  14.3 0.0 reduce-scatter.2.cloned.1.call-start
  14.4 0.1 select_reduce_fusion
  14.4 45.7 %all-gather.2.cloned.1.call-done = bf16[256,4096]{1,0:T(8,128)(2,1)} async-done(((bf16[64,4096]{1,0:T(8,128)(2,1)}), bf16[256,4096]{1,0:T(8,128)(2,1)}) %all-gather.2.cloned.1.call-update) | async-done | bytes 2097168 | tf_op jit(solution)/shard_map/all_gather | solution.py:38
  60.1 25.4 %fusion.4 = f32[256,4096]{1,0:T(8,128)} fusion(bf16[256,4096]{1,0:T(8,128)(2,1)} %all-gather.2.cloned.1.call-done, f32[4096,4096]{1,0:T(8,128)} %param.7, f32[]{:T(128)S(6)} %div.26, f32[256]{0:T(256)S(1)} %select_reduce_fusion), kind=kOutput, calls=%fused_computation.5 | convolution fusion | flops 8641314816 | bytes 73401344 | tf_op jit(solution)/shard_map/dot_general | solution.py:39
  85.5 0.0 reduce-scatter.2.cloned.1.call-update
  85.6 44.7 %reduce-scatter.2.cloned.1.call-done = f32[64,4096]{1,0:T(8,128)} async-done(((f32[256,4096]{1,0:T(8,128)}), f32[64,4096]{1,0:T(8,128)}) %reduce-scatter.2.cloned.1.call-update) | async-done | bytes 1048592 | tf_op jit(solution)/shard_map/reduce_scatter | solution.py:41
  130.3 2.1 %convert_element_type.11 = bf16[64,4096]{1,0:T(8,128)(2,1)} convert(f32[64,4096]{1,0:T(8,128)} %reduce-scatter.2.cloned.1.call-done) | non-fusion elementwise | flops 262144 | bytes 1572864 | tf_op jit(solution)/shard_map/convert_element_type | solution.py:42
  (2 shorter events, 0.0 us)
Async XLA Ops:
  6.5 53.6 %all-gather.2.cloned.1.call-start = ((), (), s32[]{:S(2)}) async-start(), calls=%async_computation.1 | async-start | bytes 2621440 | tf_op jit(solution)/shard_map/all_gather | solution.py:38
  14.3 116.0 %reduce-scatter.2.cloned.1.call-start = ((), (), s32[]{:S(2)}) async-start(), calls=%async_computation.2 | async-start | bytes 5242880 | tf_op jit(solution)/shard_map/reduce_scatter | solution.py:41
Sparse Core Ops, SparseCore 0:
  14.4 45.6 all-gather.1
  85.7 44.5 reduce-scatter.1
where the time goes:
time: 141 us; the launch traced here: 139 us
  waiting for transfers between devices  90.4 us (64%)
  matrix products  25.4 us (18%)
  between operations  14.8 us (10%)
  other arithmetic  7.83 us (6%)
    all_gather x1, waiting for transfers between devices, shards(): piece = lax.all_gather(token_q, 'col', axis=0, tiled=True)  45.7 us
    reduce_scatter x1, waiting for transfers between devices, shards(): lax.psum_scatter(partial_sum, 'row', scatter_dimension=0, tiled=True)  44.7 us
    dot_general x1, matrix products, shards(): values = jnp.dot(piece, weight_q, preferred_element_type=jnp.float32)  25.4 us
  transfers between devices with their start and end apart: 2, of which 2 were waited for; matrix products, arithmetic and copies ran while one was open for 0% of the time, Pallas kernels for 0%

commit v1 on v0

--- a/solution.py
+++ b/solution.py
@@ -1,12 +1,16 @@
+import functools
+
 import jax
 import jax.numpy as jnp
 from jax import lax
+from jax.experimental import pallas as pl
+from jax.experimental.pallas import tpu as pltpu
 from jax.sharding import PartitionSpec as P
 
 TOK_DEV = 64
-
-
 QMAX = 448.0
+MESH = pl.DeviceIdType.MESH
+MIB = 1 << 20
 
 
 def delayed_scale(history, window):
@@ -28,7 +32,7 @@
     return jnp.sum(jnp.where(onehot, table[None, :], jnp.float32(0.0)), axis=1)
 
 
-def shards(tokens, weight, token_amax, token_window, weight_amax, weight_window):
+def general(tokens, weight, token_amax, token_window, weight_amax, weight_window):
     token_scale = delayed_scale(token_amax[:, 0, :], token_window[:, 0])
     own_scale = lax.dynamic_index_in_dim(token_scale, lax.axis_index("col"), 0, keepdims=False)
     tile_scale = delayed_scale(weight_amax[0, 0, :], weight_window[0, 0])
@@ -42,7 +46,325 @@
     return summed.astype(jnp.bfloat16)
 
 
+def window_scale(history, window):
+    position = lax.broadcasted_iota(jnp.int32, history.shape, 1)
+    keep = position >= history.shape[1] - window
+    return QMAX / jnp.max(jnp.where(keep, history, 0.0), axis=1, keepdims=True)
+
+
+def fused(dims, tok_hbm, w_hbm, tam, twin, wam, wwin, out,
+          tokf, stage, wq, tq, mine, psend, prec, xsend, xrec, accb,
+          tok_sem, stage_sem, zs, zr, ps, pr, xs, xr):
+    rows, depth, wide, nstage = dims
+    half, dk = rows // 2, depth // 2
+    groups = wq.shape[0]
+    z, r = lax.axis_index("col"), lax.axis_index("row")
+    x, c = r // 2, r % 2
+    sibling, across = x * 2 + (1 - c), (1 - x) * 2 + c
+    middle = (z % 3) != 0
+
+    low = z < 2
+    zz = jnp.where(low, z, 3 - z)
+
+    def order(k):
+        b = (k + zz) % 2 if k < 2 else k
+        return jnp.where(low, b, 3 - b)
+
+    blocks = [order(k) for k in range(4)]
+
+    def stage_copy(g, kk, slot):
+        return pltpu.make_async_copy(
+            w_hbm.at[pl.ds(kk * dk, dk), pl.ds(pl.multiple_of(g * wide, wide), wide)],
+            stage.at[slot], stage_sem.at[slot])
+
+    tok_copy = pltpu.make_async_copy(tok_hbm, tokf, tok_sem)
+    tok_copy.start()
+    for i in range(nstage):
+        stage_copy(i // 2, i % 2, i).start()
+
+    barrier = pltpu.get_barrier_semaphore()
+    for who in (sibling, across):
+        pl.semaphore_signal(barrier, inc=1, device_id={"row": who}, device_id_type=MESH)
+
+    @pl.when(z > 0)
+    def _():
+        pl.semaphore_signal(barrier, inc=1, device_id={"col": z - 1}, device_id_type=MESH)
+
+    @pl.when(z < 3)
+    def _():
+        pl.semaphore_signal(barrier, inc=1, device_id={"col": z + 1}, device_id_type=MESH)
+
+    token_scale = window_scale(tam[:, 0, :], twin[...])
+    weight_scale = window_scale(wam[0], wwin[...])
+    table = 1.0 / (token_scale * weight_scale)
+    which = lax.broadcasted_iota(jnp.int32, table.shape, 0)
+
+    def pick(values, b):
+        return jnp.sum(jnp.where(which == b, values, 0.0), axis=0, keepdims=True)
+
+    own_scale = pick(token_scale, z)
+
+    def z_copy(b, p, right):
+        to = z + 1 if right else z - 1
+        piece = b * 4 + p
+        return pltpu.make_async_remote_copy(
+            src_ref=tq.at[piece], dst_ref=tq.at[piece],
+            send_sem=zs.at[int(right) * 16 + piece], recv_sem=zr.at[piece],
+            device_id={"col": to}, device_id_type=MESH)
+
+    def hop(b, p, act):
+        @pl.when(b > z)
+        def _():
+            act(z_copy(b, p, False))
+
+        @pl.when(b < z)
+        def _():
+            act(z_copy(b, p, True))
+
+    def forward(b, p):
+        @pl.when(middle)
+        def _():
+            z_copy(b, p, True).wait_recv()
+            hop(b, p, lambda copy: copy.start())
+
+    def arrive(b, p):
+        @pl.when(jnp.logical_not(middle))
+        def _():
+            z_copy(b, p, True).wait_recv()
+
+    def p_copy(slot, h, g):
+        unit = (slot * 2 + h) * groups + g
+        return pltpu.make_async_remote_copy(
+            src_ref=psend.at[unit], dst_ref=prec.at[unit],
+            send_sem=ps.at[unit], recv_sem=pr.at[unit],
+            device_id={"row": sibling}, device_id_type=MESH)
+
+    def x_copy(h, g):
+        unit = h * groups + g
+        return pltpu.make_async_remote_copy(
+            src_ref=xsend.at[unit], dst_ref=xrec.at[unit],
+            send_sem=xs.at[unit], recv_sem=xr.at[unit],
+            device_id={"row": across}, device_id_type=MESH)
+
+    def give(b, h, g, values):
+        slot = (b // 2 + x) % 2
+        unit = (slot * 2 + h) * groups + g
+
+        @pl.when(b % 2 != c)
+        def _():
+            psend[unit] = values.astype(jnp.bfloat16)
+            p_copy(slot, h, g).start()
+
+        @pl.when(b % 2 == c)
+        def _():
+            mine[unit] = values
+
+    def pair_sum(b, h, g):
+        slot = (b // 2 + x) % 2
+        unit = (slot * 2 + h) * groups + g
+
+        @pl.when(b % 2 == c)
+        def _():
+            p_copy(slot, h, g).wait_recv()
+            total = mine[unit] + prec[unit].astype(jnp.float32)
+
+            @pl.when(slot == 1)
+            def _():
+                xsend[h * groups + g] = total.astype(jnp.bfloat16)
+                x_copy(h, g).start()
+
+            @pl.when(slot == 0)
+            def _():
+                mine[unit] = total
+
+    def final_sum(h, g):
+        unit = h * groups + g
+        x_copy(h, g).wait_recv()
+        total = mine[unit] + xrec[unit].astype(jnp.float32)
+        out[pl.ds(h * half, half), pl.ds(pl.multiple_of(g * wide, wide), wide)] = total.astype(jnp.bfloat16)
+
+    def loop(body):
+        lax.fori_loop(0, groups, lambda g, carry: (body(g), carry)[1], 0)
+
+    tok_copy.wait()
+    for p in range(4):
+        h, kk = p // 2, p % 2
+        tq[z * 4 + p] = quantize(tokf[pl.ds(h * half, half), pl.ds(kk * dk, dk)], own_scale)
+        if p == 0:
+            pl.semaphore_wait(barrier, 2 + (z > 0).astype(jnp.int32) + (z < 3).astype(jnp.int32))
+
+        @pl.when(z > 0)
+        def _():
+            z_copy(z, p, False).start()
+
+        @pl.when(z < 3)
+        def _():
+            z_copy(z, p, True).start()
+
+    step_rows = 256
+    own_descale = pick(table, z)
+
+    def stream(g):
+        total = jnp.zeros((rows, wide), jnp.float32)
+        for kk in range(2):
+            i = g * 2 + kk
+            slot = i % nstage
+            stage_copy(g, kk, slot).wait()
+
+            def part(j, total):
+                at = pl.ds(pl.multiple_of(j * step_rows, step_rows), step_rows)
+                rounded = quantize(stage[slot, at, :], weight_scale)
+                wq[g, pl.ds(pl.multiple_of(kk * dk + j * step_rows, step_rows), step_rows), :] = rounded
+                lhs = jnp.concatenate([tq[z * 4 + kk, :, at], tq[z * 4 + 2 + kk, :, at]], axis=0)
+                return total + jnp.dot(lhs, rounded, preferred_element_type=jnp.float32)
+
+            total = lax.fori_loop(0, dk // step_rows, part, total)
+
+            @pl.when(i + nstage < groups * 2)
+            def _():
+                later = i + nstage
+                stage_copy_dyn(later, slot).start()
+        total = total * own_descale
+        for h in range(2):
+            give(blocks[0], h, g, total[h * half:(h + 1) * half])
+
+    def stage_copy_dyn(i, slot):
+        return pltpu.make_async_copy(
+            w_hbm.at[pl.ds(pl.multiple_of((i % 2) * dk, dk), dk),
+                     pl.ds(pl.multiple_of((i // 2) * wide, wide), wide)],
+            stage.at[slot], stage_sem.at[slot])
+
+    def stream_step(g):
+        stream(g)
+        for p in range(4):
+            @pl.when(g == p + 1)
+            def _():
+                forward(blocks[1], p)
+                forward(blocks[2], p)
+        for p in range(2):
+            @pl.when(g == groups - 2 + p)
+            def _():
+                forward(blocks[3], p)
+
+    loop(stream_step)
+    for h in range(2):
+        loop(lambda g: pair_sum(blocks[0], h, g))
+
+    for b in blocks[1:3]:
+        for p in range(4):
+            arrive(b, p)
+    scales = [pick(table, b) for b in blocks]
+
+    def two(g):
+        total = None
+        for kk in range(2):
+            lhs = jnp.concatenate([tq[b * 4 + h * 2 + kk] for b in blocks[1:3] for h in range(2)], axis=0)
+            term = jnp.dot(lhs, wq[g, pl.ds(kk * dk, dk), :], preferred_element_type=jnp.float32)
+            total = term if total is None else total + term
+        for i in range(4):
+            k, h = 1 + i // 2, i % 2
+            give(blocks[k], h, g, total[i * half:(i + 1) * half] * scales[k])
+
+    loop(two)
+    forward(blocks[3], 2)
+    forward(blocks[3], 3)
+    for k in (1, 2):
+        for h in range(2):
+            loop(lambda g: pair_sum(blocks[k], h, g))
+
+    last = blocks[3]
+    for h in range(2):
+        arrive(last, h * 2)
+
+        def first(g):
+            accb[g] = jnp.dot(tq[last * 4 + h * 2], wq[g, pl.ds(0, dk), :], preferred_element_type=jnp.float32)
+
+        loop(first)
+        arrive(last, h * 2 + 1)
+
+        def second(g):
+            total = accb[g] + jnp.dot(tq[last * 4 + h * 2 + 1], wq[g, pl.ds(dk, dk), :],
+                                      preferred_element_type=jnp.float32)
+            give(last, h, g, total * scales[3])
+
+            @pl.when(g > 0)
+            def _():
+                pair_sum(last, h, g - 1)
+
+        loop(second)
+        pair_sum(last, h, groups - 1)
+    for h in range(2):
+        loop(lambda g: final_sum(h, g))
+
+    for p in range(4):
+        @pl.when(z > 0)
+        def _():
+            z_copy(z, p, False).wait_send()
+
+        @pl.when(z < 3)
+        def _():
+            z_copy(z, p, True).wait_send()
+
+        @pl.when(middle)
+        def _():
+            for k in range(1, 4):
+                hop(blocks[k], p, lambda copy: copy.wait_send())
+    for h in range(2):
+        def sent(g):
+            p_copy(0, h, g).wait_send()
+            p_copy(1, h, g).wait_send()
+            x_copy(h, g).wait_send()
+
+        loop(sent)
+
+
+def fused_call(tokens, weight, token_amax, token_window, weight_amax, weight_window):
+    rows, depth = tokens.shape
+    columns = weight.shape[1]
+    wide, nstage = columns // 8, 3
+    groups, half, dk = 8, rows // 2, depth // 2
+    dma = pltpu.SemaphoreType.DMA
+    bf16, f32 = jnp.bfloat16, jnp.float32
+    vmem, hbm = pl.BlockSpec(memory_space=pltpu.VMEM), pl.BlockSpec(memory_space=pl.ANY)
+    return pl.pallas_call(
+        functools.partial(fused, (rows, depth, wide, nstage)),
+        out_shape=jax.ShapeDtypeStruct((rows, columns), bf16),
+        in_specs=[hbm, hbm, vmem, vmem, vmem, vmem],
+        out_specs=vmem,
+        scratch_shapes=[
+            pltpu.VMEM((rows, depth), f32),
+            pltpu.VMEM((nstage, dk, wide), f32),
+            pltpu.VMEM((groups, depth, wide), bf16),
+            pltpu.VMEM((16, half, dk), bf16),
+            pltpu.VMEM((4 * groups, half, wide), f32),
+            pltpu.VMEM((4 * groups, half, wide), bf16),
+            pltpu.VMEM((4 * groups, half, wide), bf16),
+            pltpu.VMEM((2 * groups, half, wide), bf16),
+            pltpu.VMEM((2 * groups, half, wide), bf16),
+            pltpu.VMEM((groups, half, wide), f32),
+            dma, dma((nstage,)),
+            dma((32,)), dma((16,)),
+            dma((4 * groups,)), dma((4 * groups,)),
+            dma((2 * groups,)), dma((2 * groups,)),
+        ],
+        compiler_params=pltpu.CompilerParams(
+            collective_id=0, has_side_effects=True, vmem_limit_bytes=58 * MIB),
+        cost_estimate=pl.CostEstimate(
+            flops=2 * 4 * rows * depth * columns, bytes_accessed=4 * depth * columns, transcendentals=0),
+        name="project",
+    )(tokens, weight, token_amax, token_window, weight_amax, weight_window)
+
+
 def solution(mesh):
+    def shards(tokens, weight, *scales):
+        rows, depth = tokens.shape
+        columns = weight.shape[1]
+        fits = 2 * depth * columns <= 32 * MIB and rows == TOK_DEV
+        tiles = depth % 1024 == 0 and columns % 1024 == 0
+        if mesh.shape["col"] == 4 and mesh.shape["row"] == 4 and fits and tiles:
+            return fused_call(tokens, weight, *scales)
+        return general(tokens, weight, *scales)
+
     return jax.shard_map(
         shards,
         mesh=mesh,

time: 141 us -> 66.4 us (0.47); the launches traced: 139 us -> 66.2 us
  waiting for transfers between devices: 90.4 us -> 0 us
  Pallas kernels: 0 us -> 62.4 us
  matrix products: 25.4 us -> 0 us
  between operations: 14.8 us -> 0.66 us
  other arithmetic: 7.83 us -> 0 us
  local copies, waits for them, and re-layouts: 0.67 us -> 3.18 us
    pallas_call x0 -> x1, Pallas kernels: none -> 62.4 us  [fused_call(): pl.pallas_call(functools.partial(fused, (rows, depth, wide, nstage)), out...]
    all_gather x1 -> x0, waiting for transfers between devices: 45.7 us -> none  [shards(): piece = lax.all_gather(token_q, 'col', axis=0, tiled=True)]
    reduce_scatter x1 -> x0, waiting for transfers between devices: 44.7 us -> none  [shards(): lax.psum_scatter(partial_sum, 'row', scatter_dimension=0, tiled=True)]
    dot_general x1 -> x0, matrix products: 25.4 us -> none  [shards(): values = jnp.dot(piece, weight_q, preferred_element_type=jnp.float32)]
    convert_element_type x2 -> x0, other arithmetic: 4.87 us -> none  [the longest x1 2.8 us: quantize(): return jnp.clip(values * scale, -QMAX, QMAX).astype(jnp.bfloat16)]
    unnamed x0 -> x2, local copies, waits for them, and re-layouts: none -> 3.18 us
    reduce_max x2 -> x0, other arithmetic: 2.21 us -> none  [delayed_scale(): amax = jnp.max(jnp.where(keep, history, jnp.float32(0.0)), axis=-1)]
  transfers between devices with their start and end apart: 2 -> 0, of which waited for: 2 -> 0; matrix products, arithmetic and copies ran while one was open for 0% -> 0% of each run, Pallas kernels for 0% -> 0%
where the time goes in v1:
time: 66.4 us; the launch traced here: 66.2 us
  Pallas kernels  62.4 us (94%)
  local copies, waits for them, and re-layouts  3.18 us (5%)
    pallas_call x1, Pallas kernels, fused_call(): pl.pallas_call(functools.partial(fused, (rows, depth, wide, nstage)), out...  62.4 us
    unnamed x2, local copies, waits for them, and re-layouts  3.18 us

profile of v1, /device:TPU:16, one launch (start us, length us, event | category | flops | bytes accessed | tf_op | source)
XLA Modules:
  0.0 66.2 jit_solution(12995435215345479519)
XLA Ops:
  0.7 1.3 %copy.7.twin = s32[4,1]{1,0:T(4,128)} copy(s32[4,1]{0,1:T(1,128)} %param.9) | data formatting | bytes 32 | tf_op args[3]
  2.0 62.4 %project.1 = bf16[64,4096]{1,0:T(8,128)(2,1)} custom-call(f32[64,4096]{1,0:T(8,128)} %tok_hbm.1, f32[4096,4096]{1,0:T(8,128)} %w_hbm.1, f32[4,1,16]{2,1,0:T(1,128)} %tam.1, s32[4,1]{1,0:T(4,128)} %copy.7.twin, f32[1,1,16]{2,1,0:T(1,128)} %wam.1, s32[1,1]{1,0:T(1,128)S(6)} %copy.9.wwin), custom_call_target="tpu_custom_call" | custom-call | flops 8589934592 | bytes 67108864 | tf_op jit(solution)/shard_map/project/pallas_call | solution.py:329
  64.3 1.9 %copy.10 = bf16[64,4096]{1,0:T(8,128)(2,1)} copy(bf16[64,4096]{1,0:T(8,128)(2,1)} %project.1) | data formatting | bytes 1048576

commit v2 on v1

v2 whole, which is shorter than its diff:
```python
import functools

import jax
import jax.numpy as jnp
from jax import lax
from jax.experimental import pallas as pl
from jax.experimental.pallas import tpu as pltpu
from jax.sharding import PartitionSpec as P

TOK_DEV = 64
QMAX = 448.0
MESH = pl.DeviceIdType.MESH
MIB = 1 << 20


def delayed_scale(history, window):
    hlen = history.shape[-1]
    position = jnp.arange(hlen, dtype=jnp.int32)
    keep = position >= (hlen - window)[..., None]
    amax = jnp.max(jnp.where(keep, history, jnp.float32(0.0)), axis=-1)
    return QMAX / amax


def quantize(values, scale):
    return jnp.clip(values * scale, -QMAX, QMAX).astype(jnp.bfloat16)


def row_descale(table, count):
    block_of = jnp.arange(count, dtype=jnp.int32) // TOK_DEV
    owners = jnp.arange(table.shape[0], dtype=jnp.int32)
    onehot = block_of[:, None] == owners[None, :]
    return jnp.sum(jnp.where(onehot, table[None, :], jnp.float32(0.0)), axis=1)


def general(tokens, weight, token_amax, token_window, weight_amax, weight_window):
    token_scale = delayed_scale(token_amax[:, 0, :], token_window[:, 0])
    own_scale = lax.dynamic_index_in_dim(token_scale, lax.axis_index("col"), 0, keepdims=False)
    tile_scale = delayed_scale(weight_amax[0, 0, :], weight_window[0, 0])
    token_q = quantize(tokens, own_scale)
    weight_q = quantize(weight, tile_scale)
    table = 1.0 / (token_scale * tile_scale)
    piece = lax.all_gather(token_q, "col", axis=0, tiled=True)
    values = jnp.dot(piece, weight_q, preferred_element_type=jnp.float32)
    partial_sum = values * row_descale(table, piece.shape[0])[:, None]
    summed = lax.psum_scatter(partial_sum, "row", scatter_dimension=0, tiled=True)
    return summed.astype(jnp.bfloat16)


def window_scale(history, window):
    position = lax.broadcasted_iota(jnp.int32, history.shape, 1)
    keep = position >= history.shape[1] - window
    return QMAX / jnp.max(jnp.where(keep, history, 0.0), axis=1, keepdims=True)


def fused(dims, tok_hbm, w_hbm, tam, twin, wam, wwin, out,
          tokf, stage, wq, tq, mine, psend, prec, xsend, xrec, accb,
          tok_sem, stage_sem, zs, zr, ps, pr, xs, xr):
    rows, depth, wide, nstage = dims
    dk, dq = depth // 2, depth // 4
    groups = wq.shape[0]
    z, r = lax.axis_index("col"), lax.axis_index("row")
    x, c = r // 2, r % 2
    sibling, across = x * 2 + (1 - c), (1 - x) * 2 + c
    middle = (z % 3) != 0

    low = z < 2
    zz = jnp.where(low, z, 3 - z)

    def order(k):
        b = (k + zz) % 2 if k < 2 else k
        return jnp.where(low, b, 3 - b)

    blocks = [order(k) for k in range(4)]

    def stage_copy(g, kk, slot):
        return pltpu.make_async_copy(
            w_hbm.at[pl.ds(pl.multiple_of(kk * dk, dk), dk), pl.ds(pl.multiple_of(g * wide, wide), wide)],
            stage.at[slot], stage_sem.at[slot])

    tok_copy = pltpu.make_async_copy(tok_hbm, tokf, tok_sem)
    tok_copy.start()
    barrier = pltpu.get_barrier_semaphore()
    for who in (sibling, across):
        pl.semaphore_signal(barrier, inc=1, device_id={"row": who}, device_id_type=MESH)

    @pl.when(z > 0)
    def _():
        pl.semaphore_signal(barrier, inc=1, device_id={"col": z - 1}, device_id_type=MESH)

    @pl.when(z < 3)
    def _():
        pl.semaphore_signal(barrier, inc=1, device_id={"col": z + 1}, device_id_type=MESH)

    n_blocks = twin.shape[1]
    square = (n_blocks, n_blocks)
    diagonal = lax.broadcasted_iota(jnp.int32, square, 0) == lax.broadcasted_iota(jnp.int32, square, 1)
    windows = jnp.sum(jnp.where(diagonal, jnp.broadcast_to(twin[...], square), 0), axis=1, keepdims=True)
    token_scale = window_scale(tam[:, 0, :], windows)
    weight_scale = window_scale(wam[0], wwin[...])
    table = 1.0 / (token_scale * weight_scale)
    which = lax.broadcasted_iota(jnp.int32, table.shape, 0)

    def pick(values, b):
        return jnp.sum(jnp.where(which == b, values, 0.0), axis=0, keepdims=True)

    own_scale = pick(token_scale, z)

    def z_copy(b, p, right):
        to = z + 1 if right else z - 1
        piece = b * 4 + p
        return pltpu.make_async_remote_copy(
            src_ref=tq.at[piece], dst_ref=tq.at[piece],
            send_sem=zs.at[int(right) * 16 + piece], recv_sem=zr.at[piece],
            device_id={"col": to}, device_id_type=MESH)

    def hop(b, p, act):
        @pl.when(b > z)
        def _():
            act(z_copy(b, p, False))

        @pl.when(b < z)
        def _():
            act(z_copy(b, p, True))

    def own(p, act):
        @pl.when(z > 0)
        def _():
            act(z_copy(z, p, False))

        @pl.when(z < 3)
        def _():
            act(z_copy(z, p, True))

    def begin(copy):
        copy.start()

    def left(copy):
        copy.wait_send()

    def send(n):
        if 2 <= n < 6:
            own(n - 2, left)
        if n < 4:
            own(n, begin)
        else:
            @pl.when(middle)
            def _():
                for k in (1, 2) if n < 8 else (3,):
                    z_copy(blocks[k], n % 4, True).wait_recv()
                for k in () if n < 6 else (1, 2) if n < 10 else (3,):
                    hop(blocks[k], (n - 2) % 4, left)
                for k in (1, 2) if n < 8 else (3,):
                    hop(blocks[k], n % 4, begin)

    def arrive(b, p):
        @pl.when(jnp.logical_not(middle))
        def _():
            z_copy(b, p, True).wait_recv()

    def p_copy(slot, g):
        unit = slot * groups + g
        return pltpu.make_async_remote_copy(
            src_ref=psend.at[unit], dst_ref=prec.at[unit],
            send_sem=ps.at[unit], recv_sem=pr.at[unit],
            device_id={"row": sibling}, device_id_type=MESH)

    def x_copy(g):
        return pltpu.make_async_remote_copy(
            src_ref=xsend.at[g], dst_ref=xrec.at[g],
            send_sem=xs.at[g], recv_sem=xr.at[g],
            device_id={"row": across}, device_id_type=MESH)

    def give(b, g, values):
        slot = (b // 2 + x) % 2
        unit = slot * groups + g

        @pl.when(b % 2 != c)
        def _():
            psend[unit] = values.astype(jnp.bfloat16)
            p_copy(slot, g).start()

        @pl.when(b % 2 == c)
        def _():
            mine[unit] = values

    def pair_sum(b, g):
        slot = (b // 2 + x) % 2
        unit = slot * groups + g

        @pl.when(b % 2 == c)
        def _():
            p_copy(slot, g).wait_recv()
            total = mine[unit] + prec[unit].astype(jnp.float32)

            @pl.when(slot == 1)
            def _():
                xsend[g] = total.astype(jnp.bfloat16)
                x_copy(g).start()

            @pl.when(slot == 0)
            def _():
                mine[unit] = total

    def final_sum(g):
        x_copy(g).wait_recv()
        total = mine[g] + xrec[g].astype(jnp.float32)
        out[:, pl.ds(pl.multiple_of(g * wide, wide), wide)] = total.astype(jnp.bfloat16)

    def loop(body):
        lax.fori_loop(0, groups, lambda g, carry: (body(g), carry)[1], 0)

    tok_copy.wait()
    for p in range(4):
        tq[z * 4 + p] = quantize(tokf[:, pl.ds(p * dq, dq)], own_scale)
        if p == 0:
            pl.semaphore_wait(barrier, 2 + (z > 0).astype(jnp.int32) + (z < 3).astype(jnp.int32))

        if p < 2:
            send(p)

    for i in range(nstage):
        stage_copy(i // 2, i % 2, i).start()
    step_rows = 512

    def stream_step(g):
        for kk in range(2):
            i = g * 2 + kk
            slot = i % nstage
            stage_copy(g, kk, slot).wait()

            def part(j, carry):
                at = pl.multiple_of(j * step_rows, step_rows)
                wq[g, pl.ds(pl.multiple_of(kk * dk + at, step_rows), step_rows), :] = quantize(
                    stage[slot, pl.ds(at, step_rows), :], weight_scale)
                return carry

            lax.fori_loop(0, dk // step_rows, part, 0)

            @pl.when(i + nstage < groups * 2)
            def _():
                stage_copy((i + nstage) // 2, (i + nstage) % 2, slot).start()
        for n in range(2, 8):
            @pl.when(g == n - 1)
            def _():
                send(n)

    loop(stream_step)
    scales = [pick(table, b) for b in blocks]

    def term(bs, q, g):
        lhs = jnp.concatenate([tq[b * 4 + q] for b in bs], axis=0)
        return jnp.dot(lhs, wq[g, pl.ds(q * dq, dq), :], preferred_element_type=jnp.float32)

    for p in range(4):
        arrive(blocks[1], p)

    def two(g):
        total = term(blocks[:2], 0, g)
        for q in range(1, 4):
            total += term(blocks[:2], q, g)
        for k in range(2):
            give(blocks[k], g, total[k * rows:(k + 1) * rows] * scales[k])
        for n in (8, 9):
            @pl.when(g == (n - 8) * 4 + 2)
            def _():
                send(n)

    loop(two)
    for k in range(2):
        loop(lambda g: pair_sum(blocks[k], g))

    for k in (2, 3):
        for q in range(4):
            if k == 2 and q < 2:
                send(10 + q)
            arrive(blocks[k], q)
            some = 4 if q < 3 else 2

            def quarter(n, carry):
                units = [n * some + i for i in range(some)]
                totals = [term(blocks[k:k + 1], q, g) for g in units]
                if q > 0:
                    totals = [accb[g] + total for g, total in zip(units, totals)]
                for g, total in zip(units, totals):
                    if q < 3:
                        accb[g] = total
                    else:
                        give(blocks[k], g, total * scales[k])
                if q == 3:
                    @pl.when(n > 0)
                    def _():
                        for g in units:
                            pair_sum(blocks[k], g - some)
                return carry

            lax.fori_loop(0, groups // some, quarter, 0)
        for i in range(2):
            pair_sum(blocks[k], groups - 2 + i)
    loop(final_sum)

    @pl.when(middle)
    def _():
        for p in (2, 3):
            hop(blocks[3], p, left)

    def sent(g):
        p_copy(0, g).wait_send()
        p_copy(1, g).wait_send()
        x_copy(g).wait_send()

    loop(sent)


def fused_call(tokens, weight, token_amax, token_window, weight_amax, weight_window):
    rows, depth = tokens.shape
    columns = weight.shape[1]
    wide, nstage = columns // 8, 3
    groups, dk = 8, depth // 2
    dma = pltpu.SemaphoreType.DMA
    bf16, f32 = jnp.bfloat16, jnp.float32
    vmem, hbm = pl.BlockSpec(memory_space=pltpu.VMEM), pl.BlockSpec(memory_space=pl.ANY)
    return pl.pallas_call(
        functools.partial(fused, (rows, depth, wide, nstage)),
        out_shape=jax.ShapeDtypeStruct((rows, columns), bf16),
        in_specs=[hbm, hbm, vmem, vmem, vmem, vmem],
        out_specs=vmem,
        scratch_shapes=[
            pltpu.VMEM((rows, depth), f32),
            pltpu.VMEM((nstage, dk, wide), f32),
            pltpu.VMEM((groups, depth, wide), bf16),
            pltpu.VMEM((16, rows, depth // 4), bf16),
            pltpu.VMEM((2 * groups, rows, wide), f32),
            pltpu.VMEM((2 * groups, rows, wide), bf16),
            pltpu.VMEM((2 * groups, rows, wide), bf16),
            pltpu.VMEM((groups, rows, wide), bf16),
            pltpu.VMEM((groups, rows, wide), bf16),
            pltpu.VMEM((groups, rows, wide), f32),
            dma, dma((nstage,)),
            dma((32,)), dma((16,)),
            dma((2 * groups,)), dma((2 * groups,)),
            dma((groups,)), dma((groups,)),
        ],
        compiler_params=pltpu.CompilerParams(
            collective_id=0, has_side_effects=True, vmem_limit_bytes=58 * MIB),
        cost_estimate=pl.CostEstimate(
            flops=2 * 4 * rows * depth * columns, bytes_accessed=4 * depth * columns, transcendentals=0),
        name="project",
    )(tokens, weight, token_amax, token_window.T, weight_amax, weight_window)


def solution(mesh):
    def shards(tokens, weight, *scales):
        rows, depth = tokens.shape
        columns = weight.shape[1]
        fits = 2 * depth * columns <= 32 * MIB and rows == TOK_DEV
        tiles = depth % 1024 == 0 and columns % 1024 == 0
        if mesh.shape["col"] == 4 and mesh.shape["row"] == 4 and fits and tiles:
            return fused_call(tokens, weight, *scales)
        return general(tokens, weight, *scales)

    return jax.shard_map(
        shards,
        mesh=mesh,
        in_specs=(
            P(("groups", "col"), "row"),
            P("row", "col"),
            P("groups", "row", None),
            P("groups", "row"),
            P("row", "col", None),
            P("row", "col"),
        ),
        out_specs=P(("groups", "row"), "col"),
        check_vma=False,
    )
```

time: 66.4 us -> 58.5 us (0.88)
  Pallas kernels: 62.4 us -> 55.7 us
  local copies, waits for them, and re-layouts: 3.18 us -> 1.87 us
    pallas_call x1, Pallas kernels: 62.4 us -> 55.7 us  [fused_call(): pl.pallas_call(functools.partial(fused, (rows, depth, wide, nstage)), out...]
    unnamed x2 -> x1, local copies, waits for them, and re-layouts: 3.18 us -> 1.87 us
where the time goes in v2:
time: 58.5 us; the launch traced here: 58.3 us
  Pallas kernels  55.7 us (95%)
  local copies, waits for them, and re-layouts  1.87 us (3%)
  between operations  0.66 us (1%)
    pallas_call x1, Pallas kernels, fused_call(): pl.pallas_call(functools.partial(fused, (rows, depth, wide, nstage)), out...  55.7 us
    unnamed x1, local copies, waits for them, and re-layouts  1.87 us

profile of v2, /device:TPU:16, one launch (start us, length us, event | category | flops | bytes accessed | tf_op | source)
XLA Modules:
  0.0 58.3 jit_solution(14457775324747238483)
XLA Ops:
  0.7 55.7 %project.1 = bf16[64,4096]{1,0:T(8,128)(2,1)} custom-call(f32[64,4096]{1,0:T(8,128)} %tok_hbm.1, f32[4096,4096]{1,0:T(8,128)} %w_hbm.1, f32[4,1,16]{2,1,0:T(1,128)} %tam.1, s32[1,4]{1,0:T(1,128)} %bitcast.1, f32[1,1,16]{2,1,0:T(1,128)} %wam.1, s32[1,1]{1,0:T(1,128)S(6)} %copy.8.wwin), custom_call_target="tpu_custom_call" | custom-call | flops 8589934592 | bytes 67108864 | tf_op jit(solution)/shard_map/project/pallas_call | solution.py:322
  56.4 1.9 %copy.9 = bf16[64,4096]{1,0:T(8,128)(2,1)} copy(bf16[64,4096]{1,0:T(8,128)(2,1)} %project.1) | data formatting | bytes 1048576

commit v3 on v2

--- a/solution.py
+++ b/solution.py
@@ -269,33 +269,41 @@
     for k in range(2):
         loop(lambda g: pair_sum(blocks[k], g))
 
-    for k in (2, 3):
-        for q in range(4):
-            if k == 2 and q < 2:
-                send(10 + q)
-            arrive(blocks[k], q)
-            some = 4 if q < 3 else 2
-
-            def quarter(n, carry):
+    for k, parts in ((2, ((0, 1), (2, 3))), (3, ((0, 1), (2,), (3,)))):
+        for index, part in enumerate(parts):
+            if k == 2:
+                send(10 + index)
+            for q in part:
+                arrive(blocks[k], q)
+            ends = part[-1] == 3
+            some = 2 if ends else 4 // len(part)
+
+            def portion(n, carry):
                 units = [n * some + i for i in range(some)]
-                totals = [term(blocks[k:k + 1], q, g) for g in units]
-                if q > 0:
+                totals = []
+                for g in units:
+                    total = term(blocks[k:k + 1], part[0], g)
+                    for q in part[1:]:
+                        total += term(blocks[k:k + 1], q, g)
+                    totals.append(total)
+                if index > 0:
                     totals = [accb[g] + total for g, total in zip(units, totals)]
                 for g, total in zip(units, totals):
-                    if q < 3:
+                    if ends:
+                        give(blocks[k], g, total * scales[k])
+                    else:
                         accb[g] = total
-                    else:
-                        give(blocks[k], g, total * scales[k])
-                if q == 3:
+                if ends:
                     @pl.when(n > 0)
                     def _():
                         for g in units:
                             pair_sum(blocks[k], g - some)
                 return carry
 
-            lax.fori_loop(0, groups // some, quarter, 0)
+            lax.fori_loop(0, groups // some, portion, 0)
         for i in range(2):
             pair_sum(blocks[k], groups - 2 + i)
+
     loop(final_sum)
 
     @pl.when(middle)

time: 58.5 us -> 58 us (level)
  no operation moved by 1% of the time
where the time goes in v3:
time: 58 us; the launch traced here: 57.8 us
  Pallas kernels  55.3 us (95%)
  local copies, waits for them, and re-layouts  1.87 us (3%)
  between operations  0.66 us (1%)
    pallas_call x1, Pallas kernels, fused_call(): pl.pallas_call(functools.partial(fused, (rows, depth, wide, nstage)), out...  55.3 us
    unnamed x1, local copies, waits for them, and re-layouts  1.87 us

profile of v3, /device:TPU:16, one launch (start us, length us, event | category | flops | bytes accessed | tf_op | source)
XLA Modules:
  0.0 57.8 jit_solution(17587619401991329524)
XLA Ops:
  0.7 55.3 %project.1 = bf16[64,4096]{1,0:T(8,128)(2,1)} custom-call(f32[64,4096]{1,0:T(8,128)} %tok_hbm.1, f32[4096,4096]{1,0:T(8,128)} %w_hbm.1, f32[4,1,16]{2,1,0:T(1,128)} %tam.1, s32[1,4]{1,0:T(1,128)} %bitcast.1, f32[1,1,16]{2,1,0:T(1,128)} %wam.1, s32[1,1]{1,0:T(1,128)S(6)} %copy.8.wwin), custom_call_target="tpu_custom_call" | custom-call | flops 8589934592 | bytes 67108864 | tf_op jit(solution)/shard_map/project/pallas_call | solution.py:330
  55.9 1.9 %copy.9 = bf16[64,4096]{1,0:T(8,128)(2,1)} copy(bf16[64,4096]{1,0:T(8,128)(2,1)} %project.1) | data formatting | bytes 1048576
